TPU v7x, 256 devices: a whole 4x4x8 slice. The times are simulated.
256 devices in a mesh: group: 128 (over z, y, x_hi, core), sp: 2 (over x_lo).
Axes of the slice: x: 4 (x_hi: 2, x_lo: 2; x = x_hi * 2 + x_lo), y: 4, z: 8, core: 2. Of those that a mesh axis runs over, the one named last changes fastest.
Arguments:
- query_frames: bfloat16 [1280, 64, 2560], P('group', 'sp'), may hold values from -6 to 6
- key_frames: bfloat16 [1280, 64, 2560], P('group', 'sp'), may hold values from -6 to 6
- value_frames: bfloat16 [1280, 64, 2560], P('group', 'sp'), may hold values from -6 to 6
- out_cotangent: bfloat16 [1024, 64, 2560], P('group', 'sp'), may hold values from -6 to 6
- frame_counts: int32 [128, 3], replicated, may hold values from 0 to 8, as said below
Outputs:
- attended: bfloat16 [1024, 64, 2560], P('group', 'sp')
- query_grad: bfloat16 [1280, 64, 2560], P('group', 'sp')
- key_grad: bfloat16 [1280, 64, 2560], P('group', 'sp')
- value_grad: bfloat16 [1280, 64, 2560], P('group', 'sp')
Inputs may be any that keep to these rules, and one draw needn't show every extreme that they name: `frame_counts`: row g is (a, b, c) with a + b + c = 8 and a, c at most 1, groups counted modulo 128. Anchor group g holds, from slot 0 on, the c frames of row g-1, its own b frames, then the a frames of row g+1; its remaining slots are empty. In every draw some group holds all 10 slots, sending 1 frames to each neighbour.
All inputs are finite; a program needn't handle non-finite values.
Results may differ from a plain program's by a relative error of at most 0.0072.
Values may be sent and summed in bfloat16 or wider, within the bound.
A program may use at most 64 MiB of HBM per device.

v0:
```python
import functools
import math

import jax
import jax.numpy as jnp
from jax import lax
from jax.experimental import pallas as pl
from jax.experimental.pallas import tpu as pltpu
from jax.sharding import PartitionSpec as P

HDIM = 128
MESH = pl.DeviceIdType.MESH
AHEAD_SEND = 3
AHEAD_UP = 4
AHEAD_MOVE = 6
FIRST_HEADS = 4
ROW_BLOCKS = 4


def pick(cond, yes, no):
    return lax.select_n(cond, no, yes)


def kernel(
    groups,
    counts,
    q_hbm,
    k_hbm,
    v_hbm,
    do_hbm,
    o_hbm,
    dq_hbm,
    dk_hbm,
    dv_hbm,
    raw,
    own,
    peer,
    move_src,
    move_dst,
    grads,
    back_dst,
    o_stage,
    g_stage,
    cat,
    p_buf,
    ds_buf,
    bias,
    raw_sem,
    up_sem,
    move_send,
    move_recv,
    do_send,
    do_recv,
    qkv_send,
    qkv_recv,
    back_send,
    back_recv,
    o_sem,
    g_sem,
):
    heads = own.shape[0]
    dest = own.shape[2]
    orig = raw.shape[1]
    tokens = own.shape[3]
    half = dest * tokens
    rows = 2 * half
    scaling = 1.0 / math.sqrt(HDIM)
    exponent = scaling * math.log2(math.e)

    g = lax.axis_index("group")
    s = lax.axis_index("sp")
    core = g % 2
    upper = (g + 1) % groups
    lower = (g + groups - 1) % groups
    flip = 1 - 2 * s
    to_peer = {"group": g, "sp": 1 - s}
    to_upper = {"group": upper, "sp": s + core * flip}
    to_lower = {"group": lower, "sp": s + (1 - core) * flip}

    def cols(h):
        return pl.ds(pl.multiple_of(h * HDIM, HDIM), HDIM)

    def raw_load(array, part):
        split = FIRST_HEADS * HDIM
        span = pl.ds(0, split) if part == 0 else pl.ds(split, heads * HDIM - split)
        source = (q_hbm, k_hbm, v_hbm)[array]
        return pltpu.make_async_copy(
            source.at[:, :, span], raw.at[array, :, :, span], raw_sem.at[array, part]
        )

    def up_load(h):
        return pltpu.make_async_copy(do_hbm.at[:, :, cols(h)], own.at[h, 3], up_sem.at[h])

    def move(way, h):
        return pltpu.make_async_remote_copy(
            src_ref=move_src.at[way, h],
            dst_ref=move_dst.at[way, h],
            send_sem=move_send.at[way, h],
            recv_sem=move_recv.at[way, h],
            device_id=to_upper if way == 0 else to_lower,
            device_id_type=MESH,
        )

    def do_copy(h):
        return pltpu.make_async_remote_copy(
            src_ref=own.at[h, 3],
            dst_ref=peer.at[h, 3],
            send_sem=do_send.at[h],
            recv_sem=do_recv.at[h],
            device_id=to_peer,
            device_id_type=MESH,
        )

    def qkv_copy(h):
        return pltpu.make_async_remote_copy(
            src_ref=own.at[h, pl.ds(0, 3)],
            dst_ref=peer.at[h, pl.ds(0, 3)],
            send_sem=qkv_send.at[h],
            recv_sem=qkv_recv.at[h],
            device_id=to_peer,
            device_id_type=MESH,
        )

    def back(way, h):
        return pltpu.make_async_remote_copy(
            src_ref=grads.at[h, :, dest - 1 if way == 0 else 0],
            dst_ref=back_dst.at[way, h],
            send_sem=back_send.at[way, h],
            recv_sem=back_recv.at[way, h],
            device_id=to_upper if way == 0 else to_lower,
            device_id_type=MESH,
        )

    def o_store(h):
        return pltpu.make_async_copy(o_stage.at[h], o_hbm.at[:, :, cols(h)], o_sem.at[h])

    def g_store(array, h):
        target = (dq_hbm, dk_hbm, dv_hbm)[array]
        return pltpu.make_async_copy(
            g_stage.at[h, array], target.at[:, :, cols(h)], g_sem.at[array, h]
        )

    def each(low, high, action):
        def step(h, carry):
            action(h)
            return carry

        lax.fori_loop(low, high, step, 0)

    for array in range(3):
        raw_load(array, 0).start()
    each(0, heads, lambda h: up_load(h).start())
    for array in range(3):
        raw_load(array, 1).start()

    take_low = counts[g, 0]
    native = counts[g, 1]
    take_high = counts[g, 2]
    give_low = counts[lower, 2]
    give_high = counts[upper, 0]
    shift = give_low - take_low
    last_slot = give_low + native
    from_low = take_low == 1
    from_high = take_high == 1
    swap_low = jnp.logical_and(core == 0, from_low)
    swap_high = jnp.logical_and(core == 1, from_high)

    barrier = pltpu.get_barrier_semaphore()
    for device in (to_peer, to_upper, to_lower):
        pl.semaphore_signal(barrier, inc=1, device_id=device, device_id_type=MESH)
    pl.semaphore_wait(barrier, 3)

    def send_moves(h):
        for array in range(3):
            frame = raw[array, orig - 1, :, cols(h)]
            for slot in range(dest - 2, orig - 1):
                frame = pick(last_slot == slot, raw[array, slot, :, cols(h)], frame)
            move_src[0, h, array] = frame
            move_src[1, h, array] = raw[array, 0, :, cols(h)]
        move(0, h).start()
        move(1, h).start()

    def send_up(h):
        up_load(h).wait()
        do_copy(h).start()

    def send_qkv(h):
        move(0, h).wait_recv()
        move(1, h).wait_recv()
        for array in range(3):
            for slot in range(dest):
                frame = pick(
                    shift == 1, raw[array, slot + 1, :, cols(h)], raw[array, slot, :, cols(h)]
                )
                if slot > 0:
                    frame = pick(shift == -1, raw[array, slot - 1, :, cols(h)], frame)
                else:
                    frame = pick(from_low, move_dst[0, h, array], frame)
                if slot == dest - 1:
                    frame = pick(from_high, move_dst[1, h, array], frame)
                own[h, array, slot] = frame
        qkv_copy(h).start()

    for array in range(3):
        raw_load(array, 0).wait()
    each(0, FIRST_HEADS, send_moves)
    each(0, AHEAD_UP, send_up)
    for array in range(3):
        raw_load(array, 1).wait()
    each(FIRST_HEADS, AHEAD_MOVE, send_moves)
    each(0, AHEAD_SEND, send_qkv)

    def labels(dim):
        slot = (lax.broadcasted_iota(jnp.int32, (rows, rows), dim) // tokens) % dest
        low = jnp.where(slot == 0, take_low, 0)
        high = jnp.where(slot == dest - 1, take_high, 0)
        return high - low

    bias[...] = jnp.where(labels(0) == labels(1), 0.0, -jnp.inf)

    def rows_of(ref, h, array):
        return ref[h, array].reshape(half, HDIM)

    def dot(left, right, dims):
        return lax.dot_general(
            left, right, (dims, ((), ())), preferred_element_type=jnp.float32
        )

    def compute(h):
        for array in range(3):
            cat[array, :half] = rows_of(own, h, array)
            cat[array, half:] = rows_of(peer, h, array)
        cat[3, :half] = rows_of(own, h, 3)
        cat[3, half:] = rows_of(peer, h, 3)
        for swap, slot in ((swap_low, 0), (swap_high, dest - 1)):
            mine, other = own[h, 3, slot], peer[h, 3, slot]
            cat[3, pl.ds(slot * tokens, tokens)] = pick(swap, other, mine)
            cat[3, pl.ds(half + slot * tokens, tokens)] = pick(swap, mine, other)
        size = rows // ROW_BLOCKS
        for block in range(ROW_BLOCKS):
            span = pl.ds(block * size, size)
            logits = dot(cat[0, span], cat[1], ((1,), (1,))) * exponent + bias[span]
            powers = jnp.exp2(logits - jnp.max(logits, axis=1, keepdims=True))
            softmax = powers * (1.0 / jnp.sum(powers, axis=1, keepdims=True))
            p_buf[span] = softmax.astype(jnp.bfloat16)
            prob_grad = dot(cat[3, span], cat[2], ((1,), (1,)))
            correction = jnp.sum(softmax * prob_grad, axis=1, keepdims=True)
            ds_buf[span] = (softmax * (prob_grad - correction)).astype(jnp.bfloat16)
        edge = half - tokens
        probs = jnp.concatenate(
            [
                pick(swap_low, p_buf[half : half + tokens], p_buf[:tokens]),
                p_buf[tokens:edge],
                pick(swap_high, p_buf[half + edge :], p_buf[edge:half]),
            ],
            axis=0,
        )
        shape = (dest, tokens, HDIM)
        attended = dot(probs, cat[2], ((1,), (0,)))
        o_stage[h] = attended.astype(jnp.bfloat16).reshape(shape)
        query_grad = dot(ds_buf[:half], cat[1], ((1,), (0,))) * scaling
        grads[h, 0] = query_grad.astype(jnp.bfloat16).reshape(shape)
        key_grad = dot(ds_buf[:, :half], cat[0], ((0,), (0,))) * scaling
        grads[h, 1] = key_grad.astype(jnp.bfloat16).reshape(shape)
        value_grad = dot(p_buf[:, :half], cat[3], ((0,), (0,)))
        grads[h, 2] = value_grad.astype(jnp.bfloat16).reshape(shape)

    def assemble(h):
        back(0, h).wait_recv()
        back(1, h).wait_recv()
        zero = jnp.zeros((tokens, HDIM), jnp.bfloat16)
        for array in range(3):
            for slot in range(orig):

                def source(index):
                    return grads[h, array, index] if 0 <= index < dest else zero

                frame = pick(shift == 1, source(slot - 1), source(slot))
                frame = pick(shift == -1, source(slot + 1), frame)
                inside = jnp.logical_and(slot >= give_low, slot < last_slot)
                frame = pick(inside, frame, zero)
                if slot == 0:
                    frame = pick(give_low == 1, back_dst[0, h, array], frame)
                if slot >= dest - 2:
                    top = jnp.logical_and(last_slot == slot, give_high == 1)
                    frame = pick(top, back_dst[1, h, array], frame)
                g_stage[h, array, slot] = frame
            g_store(array, h).start()

    def step(h):
        @pl.when(h + AHEAD_SEND < heads)
        def _():
            send_qkv(h + AHEAD_SEND)

        @pl.when(h + AHEAD_UP < heads)
        def _():
            send_up(h + AHEAD_UP)

        @pl.when(h + AHEAD_MOVE < heads)
        def _():
            send_moves(h + AHEAD_MOVE)

        do_copy(h).wait_recv()
        qkv_copy(h).wait_recv()
        compute(h)
        back(0, h).start()
        back(1, h).start()
        o_store(h).start()

        @pl.when(h > 0)
        def _():
            assemble(h - 1)

    each(0, heads, step)
    assemble(heads - 1)

    def finish(h):
        do_copy(h).wait_send()
        qkv_copy(h).wait_send()
        for way in range(2):
            move(way, h).wait_send()
            back(way, h).wait_send()
        o_store(h).wait()
        for array in range(3):
            g_store(array, h).wait()

    each(0, heads, finish)


def body(query_frames, key_frames, value_frames, out_cotangent, frame_counts):
    groups = lax.axis_size("group")
    orig, tokens, width = query_frames.shape
    dest = out_cotangent.shape[0]
    heads = width // HDIM
    rows = 2 * dest * tokens
    bf16 = jnp.bfloat16
    anywhere = pl.BlockSpec(memory_space=pl.ANY)
    anchor = jax.ShapeDtypeStruct((orig, tokens, width), bf16)
    attending = jax.ShapeDtypeStruct((dest, tokens, width), bf16)
    dma = pltpu.SemaphoreType.DMA
    return pl.pallas_call(
        functools.partial(kernel, groups),
        out_shape=(attending, anchor, anchor, anchor),
        in_specs=[pl.BlockSpec(memory_space=pltpu.SMEM)] + [anywhere] * 4,
        out_specs=(anywhere,) * 4,
        scratch_shapes=[
            pltpu.VMEM((3, orig, tokens, width), bf16),
            pltpu.VMEM((heads, 4, dest, tokens, HDIM), bf16),
            pltpu.VMEM((heads, 4, dest, tokens, HDIM), bf16),
            pltpu.VMEM((2, heads, 3, tokens, HDIM), bf16),
            pltpu.VMEM((2, heads, 3, tokens, HDIM), bf16),
            pltpu.VMEM((heads, 3, dest, tokens, HDIM), bf16),
            pltpu.VMEM((2, heads, 3, tokens, HDIM), bf16),
            pltpu.VMEM((heads, dest, tokens, HDIM), bf16),
            pltpu.VMEM((heads, 3, orig, tokens, HDIM), bf16),
            pltpu.VMEM((4, rows, HDIM), bf16),
            pltpu.VMEM((rows, rows), bf16),
            pltpu.VMEM((rows, rows), bf16),
            pltpu.VMEM((rows, rows), jnp.float32),
            dma((3, 2)),
            dma((heads,)),
            dma((2, heads)),
            dma((2, heads)),
            dma((heads,)),
            dma((heads,)),
            dma((heads,)),
            dma((heads,)),
            dma((2, heads)),
            dma((2, heads)),
            dma((heads,)),
            dma((3, heads)),
        ],
        compiler_params=pltpu.CompilerParams(
            collective_id=0, has_side_effects=True, vmem_limit_bytes=52 << 20
        ),
    )(frame_counts, query_frames, key_frames, value_frames, out_cotangent)


def solution(mesh):
    spread = P("group", "sp", None)
    return jax.shard_map(
        body,
        mesh=mesh,
        in_specs=(spread, spread, spread, spread, P()),
        out_specs=(spread,) * 4,
        check_vma=False,
    )
```

profile of v0, /device:TPU:2, one launch (start us, length us, event | category | flops | bytes accessed | tf_op | source)
XLA Modules:
  0.0 141.0 jit_solution(18024059334236227731)
XLA Ops:
  0.6 0.8 copy.9.counts
  1.4 132.4 %shard_map.84 = (bf16[8,32,2560]{2,1,0:T(8,128)(2,1)S(1)}, bf16[10,32,2560]{2,1,0:T(8,128)(2,1)}, bf16[10,32,2560]{2,1,0:T(8,128)(2,1)}, bf16[10,32,2560]{2,1,0:T(8,128)(2,1)}) custom-call(s32[128,3]{1,0:T(8,128)S(1)} %copy.9.counts, bf16[10,32,2560]{2,1,0:T(8,128)(2,1)} %q_hbm.1, bf16[10,32,2560]{2,1,0:T(8,128)(2,1)} %k_hbm.1, bf16[10,32,2560]{2,1,0:T(8,128)(2,1)} %v_hbm.1, ...), custom_call_target="tpu_custom_call" | custom-call | tf_op jit(solution)/shard_map/pallas_call | solution.py:341
  133.8 0.0 copy-start.2
  133.8 1.1 copy.14
  134.9 0.8 copy-done.2
  135.7 0.0 copy-start.1
  135.7 1.2 copy.15
  136.9 0.9 copy-done.1
  137.8 0.0 copy-start
  137.8 1.2 copy.16
  138.9 0.9 copy-done
  139.8 1.2 copy.17
Async XLA Ops:
  133.8 1.9 %copy-start.2 = (bf16[10,32,2560]{2,1,0:T(8,128)(2,1)S(1)}, bf16[10,32,2560]{2,1,0:T(8,128)(2,1)}, u32[]{:S(2)}) copy-start(bf16[10,32,2560]{2,1,0:T(8,128)(2,1)} %get-tuple-element.9) | copy-start | bytes 4915204
  135.7 2.0 %copy-start.1 = (bf16[10,32,2560]{2,1,0:T(8,128)(2,1)S(1)}, bf16[10,32,2560]{2,1,0:T(8,128)(2,1)}, u32[]{:S(2)}) copy-start(bf16[10,32,2560]{2,1,0:T(8,128)(2,1)} %get-tuple-element.10) | copy-start | bytes 4915204
  137.8 2.0 %copy-start = (bf16[10,32,2560]{2,1,0:T(8,128)(2,1)S(1)}, bf16[10,32,2560]{2,1,0:T(8,128)(2,1)}, u32[]{:S(2)}) copy-start(bf16[10,32,2560]{2,1,0:T(8,128)(2,1)} %get-tuple-element.11) | copy-start | bytes 4915204
where the time goes:
time: 141 us
  Pallas kernels  132 us (94%)
  local copies, waits for them, and re-layouts  7.89 us (6%)
    pallas_call x1, Pallas kernels, body(): pl.pallas_call(functools.partial(kernel, groups), out_shape=(attending, a...  132 us
    unnamed x11, local copies, waits for them, and re-layouts  7.89 us

commit v1 on v0

v1 whole, which is shorter than its diff:
```python
import functools
import math

import jax
import jax.numpy as jnp
from jax import lax
from jax.experimental import pallas as pl
from jax.experimental.pallas import tpu as pltpu
from jax.sharding import PartitionSpec as P

HDIM = 128
MESH = pl.DeviceIdType.MESH
CHUNKS = 5
AHEAD = 4
EDGE_UNROLL = 4
GATHER_FROM = 14
ROW_BLOCKS = 4


def pick(cond, yes, no):
    return lax.select_n(cond, no, yes)


def kernel(
    groups,
    counts,
    q_hbm,
    k_hbm,
    v_hbm,
    do_hbm,
    o_out,
    dq_out,
    dk_out,
    dv_out,
    raw,
    own_do,
    peer_do,
    own_edge,
    peer_edge,
    own_mid,
    peer_mid,
    move_src,
    move_dst,
    back_src,
    back_dst,
    grads,
    cat,
    p_buf,
    ds_buf,
    bias,
    raw_sem,
    up_sem,
    move_send,
    move_recv,
    do_send,
    do_recv,
    edge_send,
    edge_recv,
    mid_send,
    mid_recv,
    back_send,
    back_recv,
):
    heads = own_mid.shape[0]
    dest, tokens, _ = own_do.shape
    orig = raw.shape[1]
    inner = dest - 2
    half = dest * tokens
    rows = 2 * half
    scaling = 1.0 / math.sqrt(HDIM)
    exponent = scaling * math.log2(math.e)
    edge_slots = (0, dest - 1)
    group_heads = heads // CHUNKS

    g = lax.axis_index("group")
    s = lax.axis_index("sp")
    core = g % 2
    upper = (g + 1) % groups
    lower = (g + groups - 1) % groups
    flip = 1 - 2 * s
    to_peer = {"group": g, "sp": 1 - s}
    to_upper = {"group": upper, "sp": s + core * flip}
    to_lower = {"group": lower, "sp": s + (1 - core) * flip}

    def cols(h):
        return pl.ds(pl.multiple_of(h * HDIM, HDIM), HDIM)

    def raw_load(array):
        source = (q_hbm, k_hbm, v_hbm)[array]
        return pltpu.make_async_copy(source, raw.at[array], raw_sem.at[array])

    up_load = pltpu.make_async_copy(do_hbm, own_do, up_sem)

    def remote(src, dst, send, recv, device):
        return pltpu.make_async_remote_copy(
            src_ref=src,
            dst_ref=dst,
            send_sem=send,
            recv_sem=recv,
            device_id=device,
            device_id_type=MESH,
        )

    def move(way):
        source = move_src if way == 0 else raw.at[:, 0]
        return remote(
            source,
            move_dst.at[way],
            move_send.at[way],
            move_recv.at[way],
            to_upper if way == 0 else to_lower,
        )

    def do_copy(chunk):
        span = pl.ds(chunk * group_heads * HDIM, group_heads * HDIM)
        return remote(
            do_hbm.at[:, :, span],
            peer_do.at[:, :, span],
            do_send.at[chunk],
            do_recv.at[chunk],
            to_peer,
        )

    def edge_copy(chunk):
        span = pl.ds(chunk * group_heads, group_heads)
        return remote(
            own_edge.at[span],
            peer_edge.at[span],
            edge_send.at[chunk],
            edge_recv.at[chunk],
            to_peer,
        )

    def mid_copy(h):
        return remote(own_mid.at[h], peer_mid.at[h], mid_send.at[h], mid_recv.at[h], to_peer)

    def back(way):
        return remote(
            back_src.at[way],
            back_dst.at[way],
            back_send.at[way],
            back_recv.at[way],
            to_upper if way == 0 else to_lower,
        )

    def each(low, high, action):
        def step(h, carry):
            action(h)
            return carry

        lax.fori_loop(low, high, step, 0)

    for array in range(3):
        raw_load(array).start()
    up_load.start()

    take_low = counts[0, g]
    native = counts[1, g]
    take_high = counts[2, g]
    give_low = counts[2, lower]
    give_high = counts[0, upper]
    shift = give_low - take_low
    last_slot = give_low + native
    from_low = take_low == 1
    from_high = take_high == 1
    swap_low = jnp.logical_and(core == 0, from_low)
    swap_high = jnp.logical_and(core == 1, from_high)

    barrier = pltpu.get_barrier_semaphore()
    for device in (to_peer, to_upper, to_lower):
        pl.semaphore_signal(barrier, inc=1, device_id=device, device_id_type=MESH)
    pl.semaphore_wait(barrier, 3)

    for chunk in range(CHUNKS):
        do_copy(chunk).start()

    for array in range(3):
        raw_load(array).wait()

    def stage_move(h):
        for array in range(3):
            frame = raw[array, orig - 1, :, cols(h)]
            for slot in range(inner, orig - 1):
                frame = pick(last_slot == slot, raw[array, slot, :, cols(h)], frame)
            move_src[array, :, cols(h)] = frame

    move(1).start()
    each(0, heads, stage_move)
    move(0).start()

    def native_frame(h, array, slot):
        here = raw[array, slot, :, cols(h)]
        frame = pick(shift == 1, raw[array, slot + 1, :, cols(h)], here)
        if slot > 0:
            frame = pick(shift == -1, raw[array, slot - 1, :, cols(h)], frame)
        return frame

    def stage_mid(h):
        for array in range(3):
            for slot in range(inner):
                own_mid[h, array, slot] = native_frame(h, array, slot + 1)

    each(0, heads, stage_mid)

    def labels(dim):
        slot = (lax.broadcasted_iota(jnp.int32, (rows, rows), dim) // tokens) % dest
        low = jnp.where(slot == 0, take_low, 0)
        high = jnp.where(slot == dest - 1, take_high, 0)
        return high - low

    bias[...] = jnp.where(labels(0) == labels(1), 0.0, -jnp.inf)

    move(0).wait_recv()
    move(1).wait_recv()

    def stage_edge(h):
        for array in range(3):
            for way, (slot, moved) in enumerate(((0, from_low), (dest - 1, from_high))):
                frame = native_frame(h, array, slot)
                own_edge[h, array, way] = pick(moved, move_dst[way, array, :, cols(h)], frame)

    for chunk in range(CHUNKS):
        each(chunk * group_heads, (chunk + 1) * group_heads, stage_edge)
        edge_copy(chunk).start()

    def dot(left, right, dims):
        return lax.dot_general(
            left, right, (dims, ((), ())), preferred_element_type=jnp.float32
        )

    def attend(queries, keys, values, upstream, mask):
        logits = dot(queries, keys, ((1,), (1,))) * exponent + mask
        powers = jnp.exp2(logits - jnp.max(logits, axis=1, keepdims=True))
        softmax = powers * (1.0 / jnp.sum(powers, axis=1, keepdims=True))
        prob_grad = dot(upstream, values, ((1,), (1,)))
        correction = jnp.sum(softmax * prob_grad, axis=1, keepdims=True)
        logit_grad = softmax * (prob_grad - correction)
        return softmax.astype(jnp.bfloat16), logit_grad.astype(jnp.bfloat16)

    def edge_up(h, way):
        slot, swap = ((0, swap_low), (dest - 1, swap_high))[way]
        mine, other = own_do[slot, :, cols(h)], peer_do[slot, :, cols(h)]
        return pick(swap, other, mine), pick(swap, mine, other)

    edge_row = lax.broadcasted_iota(jnp.int32, (4 * tokens, 4 * tokens), 0) // tokens % 2
    edge_col = lax.broadcasted_iota(jnp.int32, (4 * tokens, 4 * tokens), 1) // tokens % 2
    edge_mask = jnp.where(edge_row == edge_col, 0.0, -jnp.inf)

    def edge_compute(h):
        def joined(array):
            both = [ref[h, array].reshape(2 * tokens, HDIM) for ref in (own_edge, peer_edge)]
            return jnp.concatenate(both, axis=0)

        queries, keys, values = joined(0), joined(1), joined(2)
        (low, far_low), (high, far_high) = edge_up(h, 0), edge_up(h, 1)
        upstream = jnp.concatenate([low, high, far_low, far_high], axis=0)
        probs, logit_grad = attend(queries, keys, values, upstream, edge_mask)
        mine = 2 * tokens
        query_grad = dot(logit_grad[:mine], keys, ((1,), (0,))) * scaling
        key_grad = dot(logit_grad[:, :mine], queries, ((0,), (0,))) * scaling
        value_grad = dot(probs[:, :mine], upstream, ((0,), (0,)))
        for array, grad in enumerate((query_grad, key_grad, value_grad)):
            grad = grad.astype(jnp.bfloat16)
            back_src[1, h, array] = grad[:tokens]
            back_src[0, h, array] = grad[tokens:]

    def compute(h):
        edge = half - tokens
        for array in range(3):
            for base, edges, mids in ((0, own_edge, own_mid), (half, peer_edge, peer_mid)):
                cat[array, pl.ds(base, tokens)] = edges[h, array, 0]
                cat[array, pl.ds(base + tokens, edge - tokens)] = mids[h, array].reshape(
                    edge - tokens, HDIM
                )
                cat[array, pl.ds(base + edge, tokens)] = edges[h, array, 1]
        for slot in range(1, dest - 1):
            cat[3, pl.ds(slot * tokens, tokens)] = own_do[slot, :, cols(h)]
            cat[3, pl.ds(half + slot * tokens, tokens)] = peer_do[slot, :, cols(h)]
        for way, slot in enumerate(edge_slots):
            mine, other = edge_up(h, way)
            cat[3, pl.ds(slot * tokens, tokens)] = mine
            cat[3, pl.ds(half + slot * tokens, tokens)] = other
        size = rows // ROW_BLOCKS
        for block in range(ROW_BLOCKS):
            span = pl.ds(block * size, size)
            p_buf[span], ds_buf[span] = attend(
                cat[0, span], cat[1], cat[2], cat[3, span], bias[span]
            )
        probs = jnp.concatenate(
            [
                pick(swap_low, p_buf[half : half + tokens], p_buf[:tokens]),
                p_buf[tokens:edge],
                pick(swap_high, p_buf[half + edge :], p_buf[edge:half]),
            ],
            axis=0,
        )
        shape = (dest, tokens, HDIM)
        attended = dot(probs, cat[2], ((1,), (0,)))
        o_out[:, :, cols(h)] = attended.astype(jnp.bfloat16).reshape(shape)
        query_grad = dot(ds_buf[:half], cat[1], ((1,), (0,))) * scaling
        grads[h, 0] = query_grad.astype(jnp.bfloat16).reshape(shape)
        key_grad = dot(ds_buf[:, :half], cat[0], ((0,), (0,))) * scaling
        grads[h, 1] = key_grad.astype(jnp.bfloat16).reshape(shape)
        value_grad = dot(p_buf[:, :half], cat[3], ((0,), (0,)))
        grads[h, 2] = value_grad.astype(jnp.bfloat16).reshape(shape)

    def assemble(h):
        zero = jnp.zeros((tokens, HDIM), jnp.bfloat16)
        for array in range(3):
            for slot in range(orig):

                def source(index):
                    return grads[h, array, index] if 0 <= index < dest else zero

                frame = pick(shift == 1, source(slot - 1), source(slot))
                frame = pick(shift == -1, source(slot + 1), frame)
                inside = jnp.logical_and(slot >= give_low, slot < last_slot)
                frame = pick(inside, frame, zero)
                if slot == 0:
                    frame = pick(give_low == 1, back_dst[0, h, array], frame)
                if slot >= inner:
                    top = jnp.logical_and(last_slot == slot, give_high == 1)
                    frame = pick(top, back_dst[1, h, array], frame)
                (dq_out, dk_out, dv_out)[array][slot, :, cols(h)] = frame

    up_load.wait()
    for chunk in range(CHUNKS):
        do_copy(chunk).wait_send()
    each(0, AHEAD, lambda h: mid_copy(h).start())
    for chunk in range(CHUNKS):
        do_copy(chunk).wait_recv()
    for chunk in range(CHUNKS):
        edge_copy(chunk).wait_recv()

        def edge_step(step, carry):
            for part in range(EDGE_UNROLL):
                edge_compute(step * EDGE_UNROLL + part)
            return carry

        count = group_heads // EDGE_UNROLL
        lax.fori_loop(chunk * count, (chunk + 1) * count, edge_step, 0)
    back(0).start()
    back(1).start()

    def main_step(h):
        @pl.when(h + AHEAD < heads)
        def _():
            mid_copy(h + AHEAD).start()

        mid_copy(h).wait_recv()
        compute(h)

        @pl.when(h == GATHER_FROM)
        def _():
            back(0).wait_recv()
            back(1).wait_recv()
            each(0, GATHER_FROM, assemble)

        @pl.when(h >= GATHER_FROM)
        def _():
            assemble(h)

    each(0, heads, main_step)

    for chunk in range(CHUNKS):
        edge_copy(chunk).wait_send()
    for way in range(2):
        move(way).wait_send()
        back(way).wait_send()
    each(0, heads, lambda h: mid_copy(h).wait_send())


def store_kernel(*refs):
    count = (len(refs) - 1) // 2
    sems = refs[-1]
    copies = [
        pltpu.make_async_copy(refs[i], refs[count + i], sems.at[i]) for i in range(count)
    ]
    for copy in copies:
        copy.start()
    for copy in copies:
        copy.wait()


def body(query_frames, key_frames, value_frames, out_cotangent, frame_counts):
    groups = lax.axis_size("group")
    orig, tokens, width = query_frames.shape
    dest = out_cotangent.shape[0]
    heads = width // HDIM
    rows = 2 * dest * tokens
    bf16 = jnp.bfloat16
    anywhere = pl.BlockSpec(memory_space=pl.ANY)
    in_vmem = pl.BlockSpec(memory_space=pltpu.VMEM)
    anchor = (orig, tokens, width)
    attending = (dest, tokens, width)
    dma = pltpu.SemaphoreType.DMA
    shapes = (attending, anchor, anchor, anchor)
    results = pl.pallas_call(
        functools.partial(kernel, groups),
        out_shape=tuple(pltpu.VMEM(shape, bf16) for shape in shapes),
        in_specs=[pl.BlockSpec(memory_space=pltpu.SMEM)] + [anywhere] * 4,
        out_specs=(in_vmem,) * 4,
        scratch_shapes=[
            pltpu.VMEM((3,) + anchor, bf16),
            pltpu.VMEM(attending, bf16),
            pltpu.VMEM(attending, bf16),
            pltpu.VMEM((heads, 3, 2, tokens, HDIM), bf16),
            pltpu.VMEM((heads, 3, 2, tokens, HDIM), bf16),
            pltpu.VMEM((heads, 3, dest - 2, tokens, HDIM), bf16),
            pltpu.VMEM((heads, 3, dest - 2, tokens, HDIM), bf16),
            pltpu.VMEM((3, tokens, width), bf16),
            pltpu.VMEM((2, 3, tokens, width), bf16),
            pltpu.VMEM((2, heads, 3, tokens, HDIM), bf16),
            pltpu.VMEM((2, heads, 3, tokens, HDIM), bf16),
            pltpu.VMEM((heads, 3, dest, tokens, HDIM), bf16),
            pltpu.VMEM((4, rows, HDIM), bf16),
            pltpu.VMEM((rows, rows), bf16),
            pltpu.VMEM((rows, rows), bf16),
            pltpu.VMEM((rows, rows), jnp.float32),
            dma((3,)),
            dma,
            dma((2,)),
            dma((2,)),
            dma((CHUNKS,)),
            dma((CHUNKS,)),
            dma((CHUNKS,)),
            dma((CHUNKS,)),
            dma((heads,)),
            dma((heads,)),
            dma((2,)),
            dma((2,)),
        ],
        compiler_params=pltpu.CompilerParams(
            collective_id=0, has_side_effects=True, vmem_limit_bytes=56 << 20
        ),
    )(frame_counts.T, query_frames, key_frames, value_frames, out_cotangent)
    return pl.pallas_call(
        store_kernel,
        out_shape=tuple(jax.ShapeDtypeStruct(shape, bf16) for shape in shapes),
        in_specs=[in_vmem] * 4,
        out_specs=(anywhere,) * 4,
        scratch_shapes=[dma((4,))],
        compiler_params=pltpu.CompilerParams(vmem_limit_bytes=8 << 20),
    )(*results)


def solution(mesh):
    spread = P("group", "sp", None)
    return jax.shard_map(
        body,
        mesh=mesh,
        in_specs=(spread, spread, spread, spread, P()),
        out_specs=(spread,) * 4,
        check_vma=False,
    )
```

time: 141 us -> 123 us (0.87)
  Pallas kernels: 132 us -> 122 us
  local copies, waits for them, and re-layouts: 7.89 us -> 0 us
    pallas_call x1 -> x2, Pallas kernels: 132 us -> 122 us  [the longest x1 120 us: body(): pl.pallas_call(functools.partial(kernel, groups), out_shape=tuple((pltpu....]
    unnamed x11 -> x0, local copies, waits for them, and re-layouts: 7.89 us -> none
where the time goes in v1:
time: 123 us
  Pallas kernels  122 us (99%)
    pallas_call x1, Pallas kernels, body(): pl.pallas_call(functools.partial(kernel, groups), out_shape=tuple((pltpu....  120 us
    pallas_call x1, Pallas kernels, body(): pl.pallas_call(store_kernel, out_shape=tuple((jax.ShapeDtypeStruct(shape,...  2.71 us

profile of v1, /device:TPU:2, one launch (start us, length us, event | category | flops | bytes accessed | tf_op | source)
XLA Modules:
  0.0 123.0 jit_solution(2074186682341184531)
XLA Ops:
  0.6 119.7 %shard_map.84 = (bf16[8,32,2560]{2,1,0:T(8,128)(2,1)S(1)}, bf16[10,32,2560]{2,1,0:T(8,128)(2,1)S(1)}, bf16[10,32,2560]{2,1,0:T(8,128)(2,1)S(1)}, bf16[10,32,2560]{2,1,0:T(8,128)(2,1)S(1)}) custom-call(s32[3,128]{1,0:T(4,128)} %bitcast.1, bf16[10,32,2560]{2,1,0:T(8,128)(2,1)} %q_hbm.1, bf16[10,32,2560]{2,1,0:T(8,128)(2,1)} %k_hbm.1, ...), custom_call_target="tpu_custom_call" | custom-call | tf_op jit(solution)/shard_map/pallas_call | solution.py:398
  120.3 2.7 %shard_map.85 = (bf16[8,32,2560]{2,1,0:T(8,128)(2,1)}, bf16[10,32,2560]{2,1,0:T(8,128)(2,1)}, bf16[10,32,2560]{2,1,0:T(8,128)(2,1)}, bf16[10,32,2560]{2,1,0:T(8,128)(2,1)}) custom-call(bf16[8,32,2560]{2,1,0:T(8,128)(2,1)S(1)} %get-tuple-element.8.refs_0_, bf16[10,32,2560]{2,1,0:T(8,128)(2,1)S(1)} %get-tuple-element.9.refs_1_, ...), custom_call_target="tpu_custom_call" | custom-call | tf_op jit(solution)/shard_map/pallas_call | solution.py:437

commit v2 on v1

--- a/solution.py
+++ b/solution.py
@@ -9,6 +9,8 @@
 from jax.sharding import PartitionSpec as P
 
 HDIM = 128
+SCALING = 1.0 / math.sqrt(HDIM)
+EXPONENT = SCALING * math.log2(math.e)
 MESH = pl.DeviceIdType.MESH
 CHUNKS = 5
 AHEAD = 4
@@ -21,9 +23,84 @@
     return lax.select_n(cond, no, yes)
 
 
+def dot(left, right, dims):
+    return lax.dot_general(left, right, (dims, ((), ())), preferred_element_type=jnp.float32)
+
+
+def attend(queries, keys, values, upstream, mask):
+    logits = dot(queries, keys, ((1,), (1,))) * EXPONENT + mask
+    powers = jnp.exp2(logits - jnp.max(logits, axis=1, keepdims=True))
+    softmax = powers * (1.0 / jnp.sum(powers, axis=1, keepdims=True))
+    prob_grad = dot(upstream, values, ((1,), (1,)))
+    correction = jnp.sum(softmax * prob_grad, axis=1, keepdims=True)
+    logit_grad = softmax * (prob_grad - correction)
+    return softmax.astype(jnp.bfloat16), logit_grad.astype(jnp.bfloat16)
+
+
+def attend_head(plan, shape, cat, bias, p_buf, ds_buf):
+    tokens = shape[1]
+    rows = cat.shape[1]
+    half = rows // 2
+    edge = half - tokens
+    size = rows // ROW_BLOCKS
+    for block in range(ROW_BLOCKS):
+        span = pl.ds(block * size, size)
+        p_buf[span], ds_buf[span] = attend(cat[0, span], cat[1], cat[2], cat[3, span], bias[span])
+    probs = jnp.concatenate(
+        [
+            pick(plan.swap_low, p_buf[half : half + tokens], p_buf[:tokens]),
+            p_buf[tokens:edge],
+            pick(plan.swap_high, p_buf[half + edge :], p_buf[edge:half]),
+        ],
+        axis=0,
+    )
+    attended = dot(probs, cat[2], ((1,), (0,)))
+    query_grad = dot(ds_buf[:half], cat[1], ((1,), (0,))) * SCALING
+    key_grad = dot(ds_buf[:, :half], cat[0], ((0,), (0,))) * SCALING
+    value_grad = dot(p_buf[:, :half], cat[3], ((0,), (0,)))
+    results = (attended, query_grad, key_grad, value_grad)
+    return [result.astype(jnp.bfloat16).reshape(shape) for result in results]
+
+
+class Plan:
+    def __init__(self, counts, groups):
+        g = lax.axis_index("group")
+        core = g % 2
+        upper = (g + 1) % groups
+        lower = (g + groups - 1) % groups
+        self.take_low = counts[0, g]
+        self.take_high = counts[2, g]
+        self.give_low = counts[2, lower]
+        self.give_high = counts[0, upper]
+        self.shift = self.give_low - self.take_low
+        self.last_slot = self.give_low + counts[1, g]
+        self.from_low = self.take_low == 1
+        self.from_high = self.take_high == 1
+        self.swap_low = jnp.logical_and(core == 0, self.from_low)
+        self.swap_high = jnp.logical_and(core == 1, self.from_high)
+
+
+def anchor_frame(plan, slot, dest, grad, low_back, high_back):
+    zero = jnp.zeros_like(low_back)
+
+    def source(index):
+        return grad(index) if 0 <= index < dest else zero
+
+    frame = pick(plan.shift == 1, source(slot - 1), source(slot))
+    frame = pick(plan.shift == -1, source(slot + 1), frame)
+    inside = jnp.logical_and(slot >= plan.give_low, slot < plan.last_slot)
+    frame = pick(inside, frame, zero)
+    if slot == 0:
+        frame = pick(plan.give_low == 1, low_back, frame)
+    if slot >= dest - 2:
+        top = jnp.logical_and(plan.last_slot == slot, plan.give_high == 1)
+        frame = pick(top, high_back, frame)
+    return frame
+
+
 def kernel(
     groups,
-    counts,
+    counts_hbm,
     q_hbm,
     k_hbm,
     v_hbm,
@@ -32,6 +109,10 @@
     dq_out,
     dk_out,
     dv_out,
+    cat,
+    bias,
+    last_back,
+    counts,
     raw,
     own_do,
     peer_do,
@@ -44,10 +125,10 @@
     back_src,
     back_dst,
     grads,
-    cat,
     p_buf,
     ds_buf,
-    bias,
+    ready,
+    counts_sem,
     raw_sem,
     up_sem,
     move_send,
@@ -67,8 +148,6 @@
     inner = dest - 2
     half = dest * tokens
     rows = 2 * half
-    scaling = 1.0 / math.sqrt(HDIM)
-    exponent = scaling * math.log2(math.e)
     edge_slots = (0, dest - 1)
     group_heads = heads // CHUNKS
 
@@ -150,30 +229,35 @@
 
         lax.fori_loop(low, high, step, 0)
 
+    counts_load = pltpu.make_async_copy(counts_hbm, counts, counts_sem)
+    counts_load.start()
     for array in range(3):
         raw_load(array).start()
     up_load.start()
 
-    take_low = counts[0, g]
-    native = counts[1, g]
-    take_high = counts[2, g]
-    give_low = counts[2, lower]
-    give_high = counts[0, upper]
-    shift = give_low - take_low
-    last_slot = give_low + native
-    from_low = take_low == 1
-    from_high = take_high == 1
-    swap_low = jnp.logical_and(core == 0, from_low)
-    swap_high = jnp.logical_and(core == 1, from_high)
-
     barrier = pltpu.get_barrier_semaphore()
-    for device in (to_peer, to_upper, to_lower):
-        pl.semaphore_signal(barrier, inc=1, device_id=device, device_id_type=MESH)
-    pl.semaphore_wait(barrier, 3)
+    pl.semaphore_signal(barrier, inc=1, device_id=to_peer, device_id_type=MESH)
+
+    @pl.when(core == 1)
+    def _():
+        for device in (to_upper, to_lower):
+            pl.semaphore_signal(barrier, inc=1, device_id=device, device_id_type=MESH)
+        pl.semaphore_wait(barrier, 1)
+
+    @pl.when(core == 0)
+    def _():
+        pl.semaphore_wait(barrier, 3)
 
     for chunk in range(CHUNKS):
         do_copy(chunk).start()
 
+    @pl.when(core == 0)
+    def _():
+        for device in (to_upper, to_lower):
+            pl.semaphore_signal(ready, inc=1, device_id=device, device_id_type=MESH)
+
+    counts_load.wait()
+    plan = Plan(counts, groups)
     for array in range(3):
         raw_load(array).wait()
 
@@ -181,18 +265,23 @@
         for array in range(3):
             frame = raw[array, orig - 1, :, cols(h)]
             for slot in range(inner, orig - 1):
-                frame = pick(last_slot == slot, raw[array, slot, :, cols(h)], frame)
+                frame = pick(plan.last_slot == slot, raw[array, slot, :, cols(h)], frame)
             move_src[array, :, cols(h)] = frame
 
+    each(0, heads, stage_move)
+
+    @pl.when(core == 1)
+    def _():
+        pl.semaphore_wait(ready, 2)
+
     move(1).start()
-    each(0, heads, stage_move)
     move(0).start()
 
     def native_frame(h, array, slot):
         here = raw[array, slot, :, cols(h)]
-        frame = pick(shift == 1, raw[array, slot + 1, :, cols(h)], here)
+        frame = pick(plan.shift == 1, raw[array, slot + 1, :, cols(h)], here)
         if slot > 0:
-            frame = pick(shift == -1, raw[array, slot - 1, :, cols(h)], frame)
+            frame = pick(plan.shift == -1, raw[array, slot - 1, :, cols(h)], frame)
         return frame
 
     def stage_mid(h):
@@ -204,8 +293,8 @@
 
     def labels(dim):
         slot = (lax.broadcasted_iota(jnp.int32, (rows, rows), dim) // tokens) % dest
-        low = jnp.where(slot == 0, take_low, 0)
-        high = jnp.where(slot == dest - 1, take_high, 0)
+        low = jnp.where(slot == 0, plan.take_low, 0)
+        high = jnp.where(slot == dest - 1, plan.take_high, 0)
         return high - low
 
     bias[...] = jnp.where(labels(0) == labels(1), 0.0, -jnp.inf)
@@ -215,7 +304,9 @@
 
     def stage_edge(h):
         for array in range(3):
-            for way, (slot, moved) in enumerate(((0, from_low), (dest - 1, from_high))):
+            for way, (slot, moved) in enumerate(
+                ((0, plan.from_low), (dest - 1, plan.from_high))
+            ):
                 frame = native_frame(h, array, slot)
                 own_edge[h, array, way] = pick(moved, move_dst[way, array, :, cols(h)], frame)
 
@@ -223,22 +314,8 @@
         each(chunk * group_heads, (chunk + 1) * group_heads, stage_edge)
         edge_copy(chunk).start()
 
-    def dot(left, right, dims):
-        return lax.dot_general(
-            left, right, (dims, ((), ())), preferred_element_type=jnp.float32
-        )
-
-    def attend(queries, keys, values, upstream, mask):
-        logits = dot(queries, keys, ((1,), (1,))) * exponent + mask
-        powers = jnp.exp2(logits - jnp.max(logits, axis=1, keepdims=True))
-        softmax = powers * (1.0 / jnp.sum(powers, axis=1, keepdims=True))
-        prob_grad = dot(upstream, values, ((1,), (1,)))
-        correction = jnp.sum(softmax * prob_grad, axis=1, keepdims=True)
-        logit_grad = softmax * (prob_grad - correction)
-        return softmax.astype(jnp.bfloat16), logit_grad.astype(jnp.bfloat16)
-
     def edge_up(h, way):
-        slot, swap = ((0, swap_low), (dest - 1, swap_high))[way]
+        slot, swap = ((0, plan.swap_low), (dest - 1, plan.swap_high))[way]
         mine, other = own_do[slot, :, cols(h)], peer_do[slot, :, cols(h)]
         return pick(swap, other, mine), pick(swap, mine, other)
 
@@ -256,15 +333,15 @@
         upstream = jnp.concatenate([low, high, far_low, far_high], axis=0)
         probs, logit_grad = attend(queries, keys, values, upstream, edge_mask)
         mine = 2 * tokens
-        query_grad = dot(logit_grad[:mine], keys, ((1,), (0,))) * scaling
-        key_grad = dot(logit_grad[:, :mine], queries, ((0,), (0,))) * scaling
+        query_grad = dot(logit_grad[:mine], keys, ((1,), (0,))) * SCALING
+        key_grad = dot(logit_grad[:, :mine], queries, ((0,), (0,))) * SCALING
         value_grad = dot(probs[:, :mine], upstream, ((0,), (0,)))
         for array, grad in enumerate((query_grad, key_grad, value_grad)):
             grad = grad.astype(jnp.bfloat16)
             back_src[1, h, array] = grad[:tokens]
             back_src[0, h, array] = grad[tokens:]
 
-    def compute(h):
+    def gather(h):
         edge = half - tokens
         for array in range(3):
             for base, edges, mids in ((0, own_edge, own_mid), (half, peer_edge, peer_mid)):
@@ -280,48 +357,24 @@
             mine, other = edge_up(h, way)
             cat[3, pl.ds(slot * tokens, tokens)] = mine
             cat[3, pl.ds(half + slot * tokens, tokens)] = other
-        size = rows // ROW_BLOCKS
-        for block in range(ROW_BLOCKS):
-            span = pl.ds(block * size, size)
-            p_buf[span], ds_buf[span] = attend(
-                cat[0, span], cat[1], cat[2], cat[3, span], bias[span]
-            )
-        probs = jnp.concatenate(
-            [
-                pick(swap_low, p_buf[half : half + tokens], p_buf[:tokens]),
-                p_buf[tokens:edge],
-                pick(swap_high, p_buf[half + edge :], p_buf[edge:half]),
-            ],
-            axis=0,
-        )
-        shape = (dest, tokens, HDIM)
-        attended = dot(probs, cat[2], ((1,), (0,)))
-        o_out[:, :, cols(h)] = attended.astype(jnp.bfloat16).reshape(shape)
-        query_grad = dot(ds_buf[:half], cat[1], ((1,), (0,))) * scaling
-        grads[h, 0] = query_grad.astype(jnp.bfloat16).reshape(shape)
-        key_grad = dot(ds_buf[:, :half], cat[0], ((0,), (0,))) * scaling
-        grads[h, 1] = key_grad.astype(jnp.bfloat16).reshape(shape)
-        value_grad = dot(p_buf[:, :half], cat[3], ((0,), (0,)))
-        grads[h, 2] = value_grad.astype(jnp.bfloat16).reshape(shape)
+
+    def compute(h):
+        results = attend_head(plan, (dest, tokens, HDIM), cat, bias, p_buf, ds_buf)
+        o_out[:, :, cols(h)] = results[0]
+        for array in range(3):
+            grads[h, array] = results[array + 1]
 
     def assemble(h):
-        zero = jnp.zeros((tokens, HDIM), jnp.bfloat16)
         for array in range(3):
             for slot in range(orig):
-
-                def source(index):
-                    return grads[h, array, index] if 0 <= index < dest else zero
-
-                frame = pick(shift == 1, source(slot - 1), source(slot))
-                frame = pick(shift == -1, source(slot + 1), frame)
-                inside = jnp.logical_and(slot >= give_low, slot < last_slot)
-                frame = pick(inside, frame, zero)
-                if slot == 0:
-                    frame = pick(give_low == 1, back_dst[0, h, array], frame)
-                if slot >= inner:
-                    top = jnp.logical_and(last_slot == slot, give_high == 1)
-                    frame = pick(top, back_dst[1, h, array], frame)
-                (dq_out, dk_out, dv_out)[array][slot, :, cols(h)] = frame
+                (dq_out, dk_out, dv_out)[array][slot, :, cols(h)] = anchor_frame(
+                    plan,
+                    slot,
+                    dest,
+                    lambda index, array=array: grads[h, array, index],
+                    back_dst[0, h, array],
+                    back_dst[1, h, array],
+                )
 
     up_load.wait()
     for chunk in range(CHUNKS):
@@ -348,6 +401,7 @@
             mid_copy(h + AHEAD).start()
 
         mid_copy(h).wait_recv()
+        gather(h)
         compute(h)
 
         @pl.when(h == GATHER_FROM)
@@ -360,26 +414,79 @@
         def _():
             assemble(h)
 
-    each(0, heads, main_step)
-
+    each(0, heads - 1, main_step)
+    last_back[...] = back_dst[:, heads - 1]
     for chunk in range(CHUNKS):
         edge_copy(chunk).wait_send()
     for way in range(2):
         move(way).wait_send()
         back(way).wait_send()
     each(0, heads, lambda h: mid_copy(h).wait_send())
-
-
-def store_kernel(*refs):
-    count = (len(refs) - 1) // 2
-    sems = refs[-1]
-    copies = [
-        pltpu.make_async_copy(refs[i], refs[count + i], sems.at[i]) for i in range(count)
+    mid_copy(heads - 1).wait_recv()
+    gather(heads - 1)
+
+
+def store_kernel(
+    groups,
+    counts_hbm,
+    o_in,
+    dq_in,
+    dk_in,
+    dv_in,
+    cat,
+    bias,
+    last_back,
+    o_hbm,
+    dq_hbm,
+    dk_hbm,
+    dv_hbm,
+    counts,
+    p_buf,
+    ds_buf,
+    o_last,
+    g_last,
+    counts_sem,
+    store_sem,
+    last_sem,
+):
+    dest, tokens, width = o_in.shape
+    orig = dq_in.shape[0]
+    early, late = pl.ds(0, width - HDIM), pl.ds(width - HDIM, HDIM)
+    targets = (o_hbm, dq_hbm, dk_hbm, dv_hbm)
+    counts_load = pltpu.make_async_copy(counts_hbm, counts, counts_sem)
+    counts_load.start()
+    stores = [
+        pltpu.make_async_copy(
+            source.at[:, :, early], target.at[:, :, early], store_sem.at[index]
+        )
+        for index, (source, target) in enumerate(zip((o_in, dq_in, dk_in, dv_in), targets))
     ]
-    for copy in copies:
-        copy.start()
-    for copy in copies:
-        copy.wait()
+    for store in stores:
+        store.start()
+    counts_load.wait()
+    plan = Plan(counts, groups)
+    results = attend_head(plan, (dest, tokens, HDIM), cat, bias, p_buf, ds_buf)
+    o_last[...] = results[0]
+    for array in range(3):
+        for slot in range(orig):
+            g_last[array, slot] = anchor_frame(
+                plan,
+                slot,
+                dest,
+                lambda index, array=array: results[array + 1][index],
+                last_back[0, array],
+                last_back[1, array],
+            )
+    lasts = [
+        pltpu.make_async_copy(source, target.at[:, :, late], last_sem.at[index])
+        for index, (source, target) in enumerate(
+            zip((o_last, g_last.at[0], g_last.at[1], g_last.at[2]), targets)
+        )
+    ]
+    for store in lasts:
+        store.start()
+    for store in stores + lasts:
+        store.wait()
 
 
 def body(query_frames, key_frames, value_frames, out_cotangent, frame_counts):
@@ -395,12 +502,19 @@
     attending = (dest, tokens, width)
     dma = pltpu.SemaphoreType.DMA
     shapes = (attending, anchor, anchor, anchor)
+    counts = frame_counts.T
     results = pl.pallas_call(
         functools.partial(kernel, groups),
-        out_shape=tuple(pltpu.VMEM(shape, bf16) for shape in shapes),
-        in_specs=[pl.BlockSpec(memory_space=pltpu.SMEM)] + [anywhere] * 4,
-        out_specs=(in_vmem,) * 4,
+        out_shape=tuple(pltpu.VMEM(shape, bf16) for shape in shapes)
+        + (
+            pltpu.VMEM((4, rows, HDIM), bf16),
+            pltpu.VMEM((rows, rows), jnp.float32),
+            pltpu.VMEM((2, 3, tokens, HDIM), bf16),
+        ),
+        in_specs=[anywhere] * 5,
+        out_specs=(in_vmem,) * 7,
         scratch_shapes=[
+            pltpu.SMEM((3, groups), jnp.int32),
             pltpu.VMEM((3,) + anchor, bf16),
             pltpu.VMEM(attending, bf16),
             pltpu.VMEM(attending, bf16),
@@ -413,10 +527,10 @@
             pltpu.VMEM((2, heads, 3, tokens, HDIM), bf16),
             pltpu.VMEM((2, heads, 3, tokens, HDIM), bf16),
             pltpu.VMEM((heads, 3, dest, tokens, HDIM), bf16),
-            pltpu.VMEM((4, rows, HDIM), bf16),
             pltpu.VMEM((rows, rows), bf16),
             pltpu.VMEM((rows, rows), bf16),
-            pltpu.VMEM((rows, rows), jnp.float32),
+            pltpu.SemaphoreType.REGULAR,
+            dma,
             dma((3,)),
             dma,
             dma((2,)),
@@ -431,17 +545,26 @@
             dma((2,)),
         ],
         compiler_params=pltpu.CompilerParams(
-            collective_id=0, has_side_effects=True, vmem_limit_bytes=56 << 20
+            collective_id=0, has_side_effects=True, vmem_limit_bytes=54 << 20
         ),
-    )(frame_counts.T, query_frames, key_frames, value_frames, out_cotangent)
+    )(counts, query_frames, key_frames, value_frames, out_cotangent)
     return pl.pallas_call(
-        store_kernel,
+        functools.partial(store_kernel, groups),
         out_shape=tuple(jax.ShapeDtypeStruct(shape, bf16) for shape in shapes),
-        in_specs=[in_vmem] * 4,
+        in_specs=[anywhere] + [in_vmem] * 7,
         out_specs=(anywhere,) * 4,
-        scratch_shapes=[dma((4,))],
-        compiler_params=pltpu.CompilerParams(vmem_limit_bytes=8 << 20),
-    )(*results)
+        scratch_shapes=[
+            pltpu.SMEM((3, groups), jnp.int32),
+            pltpu.VMEM((rows, rows), bf16),
+            pltpu.VMEM((rows, rows), bf16),
+            pltpu.VMEM((dest, tokens, HDIM), bf16),
+            pltpu.VMEM((3, orig, tokens, HDIM), bf16),
+            dma,
+            dma((4,)),
+            dma((4,)),
+        ],
+        compiler_params=pltpu.CompilerParams(vmem_limit_bytes=16 << 20),
+    )(counts, *results)
 
 
 def solution(mesh):

time: 123 us -> 119 us (0.967)
  Pallas kernels: 122 us -> 119 us
    pallas_call x1, Pallas kernels: 120 us -> 116 us  [body(): pl.pallas_call(functools.partial(kernel, groups), out_shape=tuple((pltpu....]
where the time goes in v2:
time: 119 us
  Pallas kernels  119 us (100%)
    pallas_call x1, Pallas kernels, body(): pl.pallas_call(functools.partial(kernel, groups), out_shape=tuple((pltpu....  116 us
    pallas_call x1, Pallas kernels, body(): pl.pallas_call(functools.partial(store_kernel, groups), out_shape=tuple((...  2.69 us

profile of v2, /device:TPU:2, one launch (start us, length us, event | category | flops | bytes accessed | tf_op | source)
XLA Modules:
  0.0 119.2 jit_solution(18364244915300261780)
XLA Ops:
  0.6 0.0 copy-start
  0.6 115.9 %shard_map.84 = (bf16[8,32,2560]{2,1,0:T(8,128)(2,1)S(1)}, bf16[10,32,2560]{2,1,0:T(8,128)(2,1)S(1)}, bf16[10,32,2560]{2,1,0:T(8,128)(2,1)S(1)}, bf16[10,32,2560...) custom-call(s32[3,128]{1,0:T(4,128)} %bitcast.1, ...), custom_call_target="tpu_custom_call" | custom-call | tf_op jit(solution)/shard_map/pallas_call | solution.py:506
  116.5 0.0 copy-done
  116.5 2.7 %shard_map.85 = (bf16[8,32,2560]{2,1,0:T(8,128)(2,1)}, bf16[10,32,2560]{2,1,0:T(8,128)(2,1)}, bf16[10,32,2560]{2,1,0:T(8,128)(2,1)}, bf16[10,32,2560]{2,1,0:T(8,128)(2,1)}) custom-call(s32[3,128]{1,0:T(4,128)S(1)} %bitcast.2, bf16[8,32,2560]{2,1,0:T(8,128)(2,1)S(1)} %get-tuple-element.11.o_in, bf16[10,32,2560]{2,1,0:T(8,128)(2,1)S(1)} %get-tuple-element.12.dq_in, ...), custom_call_target="tpu_custom_call" | custom-call | tf_op jit(solution)/shard_map/pallas_call | solution.py:551
Async XLA Ops:
  0.6 115.9 %copy-start = (s32[128,3]{0,1:T(4,128)S(1)}, s32[128,3]{0,1:T(4,128)}, u32[]{:S(2)}) copy-start(s32[128,3]{0,1:T(4,128)} %param.9) | copy-start | bytes 4612

commit v3 on v2

--- a/solution.py
+++ b/solution.py
@@ -12,9 +12,10 @@
 SCALING = 1.0 / math.sqrt(HDIM)
 EXPONENT = SCALING * math.log2(math.e)
 MESH = pl.DeviceIdType.MESH
-CHUNKS = 5
-AHEAD = 4
-EDGE_UNROLL = 4
+CHUNKS = 2
+AHEAD = 2
+PAIRS = 8
+EDGE_UNROLL = 5
 GATHER_FROM = 14
 ROW_BLOCKS = 4
 
@@ -190,15 +191,7 @@
             to_upper if way == 0 else to_lower,
         )
 
-    def do_copy(chunk):
-        span = pl.ds(chunk * group_heads * HDIM, group_heads * HDIM)
-        return remote(
-            do_hbm.at[:, :, span],
-            peer_do.at[:, :, span],
-            do_send.at[chunk],
-            do_recv.at[chunk],
-            to_peer,
-        )
+    do_copy = remote(do_hbm, peer_do, do_send, do_recv, to_peer)
 
     def edge_copy(chunk):
         span = pl.ds(chunk * group_heads, group_heads)
@@ -213,6 +206,10 @@
     def mid_copy(h):
         return remote(own_mid.at[h], peer_mid.at[h], mid_send.at[h], mid_recv.at[h], to_peer)
 
+    def pair_copy(pair):
+        span, h = pl.ds(2 * pair, 2), 2 * pair
+        return remote(own_mid.at[span], peer_mid.at[span], mid_send.at[h], mid_recv.at[h], to_peer)
+
     def back(way):
         return remote(
             back_src.at[way],
@@ -229,27 +226,29 @@
 
         lax.fori_loop(low, high, step, 0)
 
+    barrier = pltpu.get_barrier_semaphore()
+    pl.semaphore_signal(barrier, inc=1, device_id=to_peer, device_id_type=MESH)
+
+    @pl.when(core == 1)
+    def _():
+        for device in (to_upper, to_lower):
+            pl.semaphore_signal(barrier, inc=1, device_id=device, device_id_type=MESH)
+
     counts_load = pltpu.make_async_copy(counts_hbm, counts, counts_sem)
     counts_load.start()
     for array in range(3):
         raw_load(array).start()
     up_load.start()
 
-    barrier = pltpu.get_barrier_semaphore()
-    pl.semaphore_signal(barrier, inc=1, device_id=to_peer, device_id_type=MESH)
-
     @pl.when(core == 1)
     def _():
-        for device in (to_upper, to_lower):
-            pl.semaphore_signal(barrier, inc=1, device_id=device, device_id_type=MESH)
         pl.semaphore_wait(barrier, 1)
 
     @pl.when(core == 0)
     def _():
         pl.semaphore_wait(barrier, 3)
 
-    for chunk in range(CHUNKS):
-        do_copy(chunk).start()
+    do_copy.start()
 
     @pl.when(core == 0)
     def _():
@@ -341,14 +340,18 @@
             back_src[1, h, array] = grad[:tokens]
             back_src[0, h, array] = grad[tokens:]
 
+    def gather_mid(h, base, mids):
+        for array in range(3):
+            cat[array, pl.ds(base + tokens, inner * tokens)] = mids[h, array].reshape(
+                inner * tokens, HDIM
+            )
+
     def gather(h):
         edge = half - tokens
-        for array in range(3):
-            for base, edges, mids in ((0, own_edge, own_mid), (half, peer_edge, peer_mid)):
+        gather_mid(h, 0, own_mid)
+        for array in range(3):
+            for base, edges in ((0, own_edge), (half, peer_edge)):
                 cat[array, pl.ds(base, tokens)] = edges[h, array, 0]
-                cat[array, pl.ds(base + tokens, edge - tokens)] = mids[h, array].reshape(
-                    edge - tokens, HDIM
-                )
                 cat[array, pl.ds(base + edge, tokens)] = edges[h, array, 1]
         for slot in range(1, dest - 1):
             cat[3, pl.ds(slot * tokens, tokens)] = own_do[slot, :, cols(h)]
@@ -377,11 +380,9 @@
                 )
 
     up_load.wait()
-    for chunk in range(CHUNKS):
-        do_copy(chunk).wait_send()
-    each(0, AHEAD, lambda h: mid_copy(h).start())
-    for chunk in range(CHUNKS):
-        do_copy(chunk).wait_recv()
+    do_copy.wait_send()
+    each(0, AHEAD, lambda pair: pair_copy(pair).start())
+    do_copy.wait_recv()
     for chunk in range(CHUNKS):
         edge_copy(chunk).wait_recv()
 
@@ -396,12 +397,27 @@
     back(1).start()
 
     def main_step(h):
-        @pl.when(h + AHEAD < heads)
+        gather(h)
+
+        @pl.when(jnp.logical_and(h < 2 * PAIRS, h % 2 == 0))
         def _():
-            mid_copy(h + AHEAD).start()
-
-        mid_copy(h).wait_recv()
-        gather(h)
+            pair = h // 2
+
+            @pl.when(pair + AHEAD < PAIRS)
+            def _():
+                pair_copy(pair + AHEAD).start()
+
+            pair_copy(pair).wait_recv()
+
+        @pl.when(h == 2 * PAIRS - 6)
+        def _():
+            each(2 * PAIRS, heads, lambda late: mid_copy(late).start())
+
+        @pl.when(h >= 2 * PAIRS)
+        def _():
+            mid_copy(h).wait_recv()
+
+        gather_mid(h, half, peer_mid)
         compute(h)
 
         @pl.when(h == GATHER_FROM)
@@ -416,14 +432,16 @@
 
     each(0, heads - 1, main_step)
     last_back[...] = back_dst[:, heads - 1]
+    gather(heads - 1)
     for chunk in range(CHUNKS):
         edge_copy(chunk).wait_send()
     for way in range(2):
         move(way).wait_send()
         back(way).wait_send()
-    each(0, heads, lambda h: mid_copy(h).wait_send())
+    each(0, PAIRS, lambda pair: pair_copy(pair).wait_send())
+    each(2 * PAIRS, heads, lambda h: mid_copy(h).wait_send())
     mid_copy(heads - 1).wait_recv()
-    gather(heads - 1)
+    gather_mid(heads - 1, half, peer_mid)
 
 
 def store_kernel(
@@ -535,8 +553,8 @@
             dma,
             dma((2,)),
             dma((2,)),
-            dma((CHUNKS,)),
-            dma((CHUNKS,)),
+            dma,
+            dma,
             dma((CHUNKS,)),
             dma((CHUNKS,)),
             dma((heads,)),

time: 119 us -> 120 us (level)
  no operation moved by 1% of the time
where the time goes in v3:
time: 120 us
  Pallas kernels  119 us (99%)
    pallas_call x1, Pallas kernels, body(): pl.pallas_call(functools.partial(kernel, groups), out_shape=tuple((pltpu....  116 us
    pallas_call x1, Pallas kernels, body(): pl.pallas_call(functools.partial(store_kernel, groups), out_shape=tuple((...  2.69 us

profile of v3, /device:TPU:2, one launch (start us, length us, event | category | flops | bytes accessed | tf_op | source)
XLA Modules:
  0.0 119.8 jit_solution(9642377576752558622)
XLA Ops:
  0.6 0.0 copy-start
  0.6 116.5 %shard_map.84 = (bf16[8,32,2560]{2,1,0:T(8,128)(2,1)S(1)}, bf16[10,32,2560]{2,1,0:T(8,128)(2,1)S(1)}, bf16[10,32,2560]{2,1,0:T(8,128)(2,1)S(1)}, bf16[10,32,2560...) custom-call(s32[3,128]{1,0:T(4,128)} %bitcast.1, ...), custom_call_target="tpu_custom_call" | custom-call | tf_op jit(solution)/shard_map/pallas_call | solution.py:524
  117.1 0.0 copy-done
  117.2 2.7 %shard_map.85 = (bf16[8,32,2560]{2,1,0:T(8,128)(2,1)}, bf16[10,32,2560]{2,1,0:T(8,128)(2,1)}, bf16[10,32,2560]{2,1,0:T(8,128)(2,1)}, bf16[10,32,2560]{2,1,0:T(8,128)(2,1)}) custom-call(s32[3,128]{1,0:T(4,128)S(1)} %bitcast.2, bf16[8,32,2560]{2,1,0:T(8,128)(2,1)S(1)} %get-tuple-element.11.o_in, bf16[10,32,2560]{2,1,0:T(8,128)(2,1)S(1)} %get-tuple-element.12.dq_in, ...), custom_call_target="tpu_custom_call" | custom-call | tf_op jit(solution)/shard_map/pallas_call | solution.py:569
Async XLA Ops:
  0.6 116.5 %copy-start = (s32[128,3]{0,1:T(4,128)S(1)}, s32[128,3]{0,1:T(4,128)}, u32[]{:S(2)}) copy-start(s32[128,3]{0,1:T(4,128)} %param.9) | copy-start | bytes 4612

commit v4 on v3

--- a/solution.py
+++ b/solution.py
@@ -16,7 +16,7 @@
 AHEAD = 2
 PAIRS = 8
 EDGE_UNROLL = 5
-GATHER_FROM = 14
+GATHER_FROM = 8
 ROW_BLOCKS = 4
 
 

time: 120 us -> 119 us (level)
  no operation moved by 1% of the time
where the time goes in v4:
time: 119 us
  Pallas kernels  118 us (99%)
    pallas_call x1, Pallas kernels, body(): pl.pallas_call(functools.partial(kernel, groups), out_shape=tuple((pltpu....  116 us
    pallas_call x1, Pallas kernels, body(): pl.pallas_call(functools.partial(store_kernel, groups), out_shape=tuple((...  2.69 us

profile of v4, /device:TPU:2, one launch (start us, length us, event | category | flops | bytes accessed | tf_op | source)
XLA Modules:
  0.0 119.1 jit_solution(418110736146529830)
XLA Ops:
  0.6 0.0 copy-start
  0.6 115.7 %shard_map.84 = (bf16[8,32,2560]{2,1,0:T(8,128)(2,1)S(1)}, bf16[10,32,2560]{2,1,0:T(8,128)(2,1)S(1)}, bf16[10,32,2560]{2,1,0:T(8,128)(2,1)S(1)}, bf16[10,32,2560...) custom-call(s32[3,128]{1,0:T(4,128)} %bitcast.1, ...), custom_call_target="tpu_custom_call" | custom-call | tf_op jit(solution)/shard_map/pallas_call | solution.py:524
  116.4 0.0 copy-done
  116.4 2.7 %shard_map.85 = (bf16[8,32,2560]{2,1,0:T(8,128)(2,1)}, bf16[10,32,2560]{2,1,0:T(8,128)(2,1)}, bf16[10,32,2560]{2,1,0:T(8,128)(2,1)}, bf16[10,32,2560]{2,1,0:T(8,128)(2,1)}) custom-call(s32[3,128]{1,0:T(4,128)S(1)} %bitcast.2, bf16[8,32,2560]{2,1,0:T(8,128)(2,1)S(1)} %get-tuple-element.11.o_in, bf16[10,32,2560]{2,1,0:T(8,128)(2,1)S(1)} %get-tuple-element.12.dq_in, ...), custom_call_target="tpu_custom_call" | custom-call | tf_op jit(solution)/shard_map/pallas_call | solution.py:569
Async XLA Ops:
  0.6 115.7 %copy-start = (s32[128,3]{0,1:T(4,128)S(1)}, s32[128,3]{0,1:T(4,128)}, u32[]{:S(2)}) copy-start(s32[128,3]{0,1:T(4,128)} %param.9) | copy-start | bytes 4612

commit v5 on v4

--- a/solution.py
+++ b/solution.py
@@ -14,7 +14,7 @@
 MESH = pl.DeviceIdType.MESH
 CHUNKS = 2
 AHEAD = 2
-PAIRS = 8
+PAIRS = 7
 EDGE_UNROLL = 5
 GATHER_FROM = 8
 ROW_BLOCKS = 4

time: 119 us -> 119 us (level)
  no operation moved by 1% of the time
where the time goes in v5:
time: 119 us
  Pallas kernels  118 us (99%)
    pallas_call x1, Pallas kernels, body(): pl.pallas_call(functools.partial(kernel, groups), out_shape=tuple((pltpu....  116 us
    pallas_call x1, Pallas kernels, body(): pl.pallas_call(functools.partial(store_kernel, groups), out_shape=tuple((...  2.69 us

profile of v5, /device:TPU:2, one launch (start us, length us, event | category | flops | bytes accessed | tf_op | source)
XLA Modules:
  0.0 119.1 jit_solution(13112839372866589394)
XLA Ops:
  0.6 0.0 copy-start
  0.6 115.7 %shard_map.84 = (bf16[8,32,2560]{2,1,0:T(8,128)(2,1)S(1)}, bf16[10,32,2560]{2,1,0:T(8,128)(2,1)S(1)}, bf16[10,32,2560]{2,1,0:T(8,128)(2,1)S(1)}, bf16[10,32,2560...) custom-call(s32[3,128]{1,0:T(4,128)} %bitcast.1, ...), custom_call_target="tpu_custom_call" | custom-call | tf_op jit(solution)/shard_map/pallas_call | solution.py:524
  116.4 0.0 copy-done
  116.4 2.7 %shard_map.85 = (bf16[8,32,2560]{2,1,0:T(8,128)(2,1)}, bf16[10,32,2560]{2,1,0:T(8,128)(2,1)}, bf16[10,32,2560]{2,1,0:T(8,128)(2,1)}, bf16[10,32,2560]{2,1,0:T(8,128)(2,1)}) custom-call(s32[3,128]{1,0:T(4,128)S(1)} %bitcast.2, bf16[8,32,2560]{2,1,0:T(8,128)(2,1)S(1)} %get-tuple-element.11.o_in, bf16[10,32,2560]{2,1,0:T(8,128)(2,1)S(1)} %get-tuple-element.12.dq_in, ...), custom_call_target="tpu_custom_call" | custom-call | tf_op jit(solution)/shard_map/pallas_call | solution.py:569
Async XLA Ops:
  0.6 115.7 %copy-start = (s32[128,3]{0,1:T(4,128)S(1)}, s32[128,3]{0,1:T(4,128)}, u32[]{:S(2)}) copy-start(s32[128,3]{0,1:T(4,128)} %param.9) | copy-start | bytes 4612
